TPU v7x, 32 devices: a whole 2x2x4 slice. The times are simulated.
32 devices in a mesh: band: 2 (over x), tm: 2 (over core), inp: 8 (over z, y).
Axes of the slice: x: 2, y: 2, z: 4, core: 2. Of those that a mesh axis runs over, the one named last changes fastest.
Arguments:
- samples: int32 [1024, 131072], P('inp', ('band', 'tm')), parts along dimension 1, may hold values from -128 to 127
- flags: int32 [2048], P(('band', 'inp')), parts along dimension 0, may hold values 0 or 1
Outputs:
- visibilities: bfloat16 [256, 2, 1024, 1024], P(('band', 'inp'), None, None, 'tm'), parts along dimension 0
There are 2 independent parts, one for each index of `band`. A program takes and returns all parts, laid end to end along the dimension named above; each array names one. Nothing has to cross between parts.
Inputs may be any that keep to these rules, and one draw needn't show every extreme that they name: `samples`: whole numbers.
All inputs are finite; a program needn't handle non-finite values. No bound on the sum of `flags` on one device may be relied on, other than what follows from the above.
Results may differ from a plain program's by a relative error of at most 0.0056.
Values may be sent and summed in bfloat16 or wider, within the bound.
No kernel may reach another device: no remote copies, remote signals or barrier semaphores. Data moves between devices by JAX's collectives and lax.ppermute only.
A program may use at most 128 MiB of HBM per device.

v0:
```python
import math

import jax
import jax.numpy as jnp
from jax import lax
from jax.sharding import PartitionSpec as P

NFFT = 1024
TAPS = 4
CH_FIRST = 384
CH = 128


def passed_along(value, axis, by):
    length = lax.axis_size(axis)
    pairs = [(i, i + by) for i in range(length) if 0 <= i + by < length]
    return lax.ppermute(value, axis, pairs)


def window_table():
    positions = jnp.arange(TAPS * NFFT, dtype=jnp.float32) + 0.5
    shaped = jnp.sinc((positions - TAPS * NFFT / 2) / NFFT)
    taper = 0.5 - 0.5 * jnp.cos(2 * math.pi * positions / (TAPS * NFFT))
    return (shaped * taper).reshape(TAPS, NFFT)


def transform_table():
    sample_idx = jnp.arange(NFFT, dtype=jnp.int32)
    chan_idx = CH_FIRST + jnp.arange(CH, dtype=jnp.int32)
    angles = (sample_idx[:, None] * chan_idx[None, :] % NFFT).astype(jnp.float32) * (
        2 * math.pi / NFFT
    )
    both = jnp.stack([jnp.cos(angles), -jnp.sin(angles)], axis=1) / math.sqrt(NFFT)
    return both.reshape(NFFT, 2 * CH)


def filter_bank(extended, window, frames):
    summed = jnp.zeros((extended.shape[0], frames, NFFT), jnp.float32)
    for tap_index in range(TAPS):
        begin = TAPS - 1 - tap_index
        summed = summed + window[tap_index] * extended[:, begin : begin + frames]
    return summed


def transform(filtered, table):
    rows, frames, width = filtered.shape
    out = jnp.dot(
        filtered.reshape(rows * frames, width),
        table,
        precision=lax.Precision.HIGHEST,
        preferred_element_type=jnp.float32,
    )
    return out.reshape(rows, frames, 2, CH)


def correlate(left_side, right_side):
    chans, frames, _, row_count = left_side.shape
    depth = 2 * frames
    real_rows = left_side.reshape(chans, depth, row_count)
    imag_rows = jnp.stack([left_side[:, :, 1], -left_side[:, :, 0]], axis=2).reshape(
        chans, depth, row_count
    )
    left_both = jnp.stack([real_rows, imag_rows], axis=1)
    right_rows = right_side.reshape(chans, depth, right_side.shape[3])
    out = jnp.einsum("crka,ckb->crab", left_both, right_rows, preferred_element_type=jnp.float32)
    return out.astype(jnp.bfloat16)


def local(samples, flags):
    row_count = samples.shape[0]
    frames_dev = samples.shape[1] // NFFT
    window = window_table()
    table = transform_table()
    voltage = (
        (samples.astype(jnp.float32) / 128.0)
        .astype(jnp.bfloat16)
        .reshape(row_count, frames_dev, NFFT)
    )
    local_volts = voltage.astype(jnp.float32)
    leading = jnp.zeros((row_count, TAPS - 1, NFFT), jnp.float32)
    spectra = transform(
        filter_bank(jnp.concatenate([leading, local_volts], axis=1), window, frames_dev), table
    )
    weight = flags.astype(jnp.float32)[:, None, None, None]
    received = passed_along(voltage[:, frames_dev - (TAPS - 1) :], "tm", 1)
    source = jnp.concatenate([received.astype(jnp.float32), leading], axis=1)
    tail_part = transform(filter_bank(source, window, TAPS - 1), table)
    spectra = spectra.at[:, : TAPS - 1].add(tail_part)
    channels = (spectra * weight).astype(jnp.bfloat16).transpose(3, 1, 2, 0)
    timed = lax.all_gather(channels, "tm", axis=1, tiled=True)
    left_all = lax.all_to_all(timed, "inp", split_axis=0, concat_axis=3, tiled=True)
    total_inputs = left_all.shape[3]
    half_width = total_inputs // lax.axis_size("tm")
    right_side = lax.dynamic_slice_in_dim(
        left_all, lax.axis_index("tm") * half_width, half_width, 3
    )
    return correlate(left_all, right_side)


def solution(mesh):
    return jax.shard_map(
        local,
        mesh=mesh,
        in_specs=(P("inp", ("band", "tm")), P(("band", "inp"))),
        out_specs=P(("band", "inp"), None, None, "tm"),
        check_vma=False,
    )
```

profile of v0, /device:TPU:0, one launch (start us, length us, event | category | flops | bytes accessed | tf_op | source)
XLA Modules:
  0.0 252.5 jit_solution(2288556194103495680)
XLA Ops:
  6.5 6.6 %multiply_convert_fusion = bf16[128,32768]{1,0:T(8,128)(2,1)S(1)} fusion(s32[128,32768]{1,0:T(8,128)} %param.4), kind=kLoop, calls=%fused_computation.13 | loop fusion | flops 12582912 | bytes 25165824 | tf_op jit(solution)/shard_map/convert_element_type | solution.py:76
  13.1 7.1 %copy_bitcast_fusion = (bf16[128,32,1024]{2,0,1:T(8,128)(2,1)S(1)}, f32[128,32,1024]{2,0,1:T(8,128)}) fusion(bf16[16,32,8,1024]{3,2,1,0:T(8,128)(2,1)S(1)} %bitcast.46), kind=kLoop, calls=%fused_computation.14 | loop fusion | flops 4194304 | bytes 33554432 | tf_op jit(solution)/shard_map/reshape | solution.py:77
  20.3 0.1 slice.99
  20.3 2.4 collective-permute-start
  22.8 0.1 fusion.57
  22.9 2.1 fusion.52
  25.0 0.0 copy-start.2
  25.0 23.9 %fusion.5 = f32[128,32,2,128]{3,0,2,1:T(8,128)S(1)} fusion(f32[128,32,1024]{2,0,1:T(8,128)} %get-tuple-element.18, f32[1024]{0:T(1024)S(1)} %get-tuple-element.22, f32[1024]{0:T(1024)S(1)} %get-tuple-element.23, f32[1024]{0:T(1024)S(1)} %get-tuple-element.24, f32[1024]{0:T(1024)S(1)} %get-tuple-element.25, f32[1024,1,128]{0,2,1:T(8,128)S(1)} %get-tuple-element.27, ...), kind=kOutput, calls=%fused_computation.9 | convolution fusion | flops 12914786304 | bytes 22036480 | tf_op jit(solution)/shard_map/dot_general | solution.py:47
  49.0 0.2 convert_element_type.46
  49.2 1.7 fusion.34
  50.9 0.6 fusion.19
  51.5 2.9 %copy.18 = bf16[128,32,2,128]{3,0,2,1:T(8,128)(2,1)} copy(bf16[128,32,2,128]{0,3,2,1:T(8,128)(2,1)S(1)} %fusion.19) | data formatting | bytes 4194304 | tf_op jit(solution)/shard_map/transpose | solution.py:89
  54.4 0.0 all-gather.2.cloned.1.call-update
  54.4 15.9 %all-gather.2.cloned.1.call-done = bf16[128,64,2,128]{3,0,2,1:T(8,128)(2,1)} async-done(((bf16[128,32,2,128]{3,0,2,1:T(8,128)(2,1)}), bf16[128,64,2,128]{3,0,2,1:T(8,128)(2,1)}) %all-gather.2.cloned.1.call-update) | async-done | bytes 4194320 | tf_op jit(solution)/shard_map/all_gather | solution.py:90
  70.3 8.5 %copy.19 = bf16[128,64,2,128]{3,2,1,0:T(2,128)(2,1)} copy(bf16[128,64,2,128]{3,0,2,1:T(8,128)(2,1)} %all-gather.2.cloned.1.call-done) | data formatting | bytes 8388608 | tf_op jit(solution)/shard_map/all_gather | solution.py:90
  78.9 5.8 %all-to-all-start = ((bf16[128,64,2,128]{3,2,1,0:T(2,128)(2,1)}), bf16[128,64,2,128]{3,2,1,0:T(2,128)(2,1)}, u32[]{:S(2)}, u32[]{:S(2)}) async-start(bf16[128,64,2,128]{3,2,1,0:T(2,128)(2,1)} %copy.19), calls=%async_computation | async-start | bytes 8388608 | tf_op jit(solution)/shard_map/all_to_all | solution.py:91
  84.6 93.7 %all-to-all-done = bf16[128,64,2,128]{3,2,1,0:T(2,128)(2,1)} async-done(((bf16[128,64,2,128]{3,2,1,0:T(2,128)(2,1)}), bf16[128,64,2,128]{3,2,1,0:T(2,128)(2,1)}, u32[]{:S(2)}, u32[]{:S(2)}) %all-to-all-start) | async-done | bytes 4194336 | tf_op jit(solution)/shard_map/all_to_all | solution.py:91
  178.4 3.4 %copy.20 = bf16[128,64,2,128]{3,1,2,0:T(8,128)(2,1)S(1)} copy(bf16[128,64,2,128]{3,2,1,0:T(2,128)(2,1)} %all-to-all-done) | data formatting | bytes 8388608 | tf_op jit(solution)/shard_map/all_to_all | solution.py:91
  181.8 0.0 copy-start
  181.8 2.0 copy-done
  183.8 5.6 %copy.21 = bf16[16,64,2,8,128]{4,3,2,1,0:T(8,128)(2,1)} copy(bf16[16,64,2,8,128]{4,1,2,0,3:T(8,128)(2,1)S(1)} %bitcast.44) | data formatting | bytes 8388608 | tf_op jit(solution)/shard_map/all_to_all | solution.py:91
  189.4 7.4 %stack_reshape.6 = bf16[16,1,128,1024]{3,2,0,1:T(8,128)(2,1)} reshape(bf16[16,64,2,8,128]{4,3,2,1,0:T(8,128)(2,1)} %copy.21) | data formatting | bytes 8388608 | tf_op jit(solution)/shard_map/stack;reshape | solution.py:63
  196.8 6.4 %copy.24 = bf16[16,1,128,1024]{2,3,1,0:T(8,128)(2,1)} copy(bf16[16,1,128,1024]{3,2,0,1:T(8,128)(2,1)} %stack_reshape.6) | data formatting | bytes 8388608 | tf_op jit(solution)/shard_map/stack;reshape | solution.py:63
  203.2 3.3 %copy.36 = bf16[8,16,2,8,8,128]{5,4,0,3,2,1:T(8,128)(2,1)S(1)} copy(bf16[8,16,2,8,8,128]{5,4,3,2,1,0:T(8,128)(2,1)} %bitcast.45) | data formatting | bytes 8388608 | tf_op jit(solution)/shard_map/all_to_all | solution.py:91
  206.5 2.3 fusion.90
  208.8 0.3 constant_dynamic-slice_fusion
  209.1 2.2 copy.26
  211.3 2.3 reshape.177
  213.5 2.6 %pad_maximum_fusion = bf16[16,64,2,1024]{3,1,2,0:T(8,128)(2,1)S(1)} fusion(bf16[16,64,1,1024]{3,1,2,0:T(8,128)(2,1)} %get-tuple-element.20, bf16[16,64,1,1024]{3,1,2,0:T(8,128)(2,1)} %get-tuple-element.19), kind=kLoop, calls=%fused_computation.23 | loop fusion | flops 2097152 | bytes 8388608 | tf_op jit(solution)/shard_map/stack | solution.py:60
  216.1 4.3 %copy.23 = bf16[16,64,2,1024]{3,0,2,1:T(8,128)(2,1)} copy(bf16[16,64,2,1024]{3,1,2,0:T(8,128)(2,1)S(1)} %pad_maximum_fusion) | data formatting | bytes 8388608 | tf_op jit(solution)/shard_map/stack | solution.py:60
  220.5 6.7 %copy.25 = bf16[16,1,128,1024]{2,3,1,0:T(8,128)(2,1)} copy(bf16[16,1,128,1024]{3,0,2,1:T(8,128)(2,1)} %bitcast.49) | data formatting | bytes 8388608 | tf_op jit(solution)/shard_map/stack;reshape | solution.py:63
  227.2 18.4 %convolution_convert_fusion = bf16[16,2,1024,512]{3,2,1,0:T(8,128)(2,1)} fusion(bf16[16,1,128,1024]{2,3,1,0:T(8,128)(2,1)} %copy.25, bf16[16,1,128,1024]{2,3,1,0:T(8,128)(2,1)} %copy.24, bf16[16,128,512,1]{2,1,0,3:T(8,128)(2,1)S(1)} %copy-done.1), kind=kOutput, calls=%fused_computation | convolution fusion | flops 4315938816 | bytes 44040192 | tf_op jit(solution)/shard_map/crka,ckb->crab/dot_general | solution.py:65
  (8 shorter events, 0.0 us)
Async XLA Ops:
  6.5 63.8 %all-gather.2.cloned.1.call-start = ((), (), s32[]{:S(2)}) async-start(), calls=%async_computation.1 | async-start | bytes 6291456 | tf_op jit(solution)/shard_map/all_gather | solution.py:90
  20.3 28.6 %collective-permute-start = (bf16[128,3,1024]{2,0,1:T(8,128)(2,1)S(1)}, bf16[128,3,1024]{2,0,1:T(8,128)(2,1)S(1)}, u32[]{:S(2)}, u32[]{:S(2)}) collective-permute-start(bf16[128,3,1024]{2,0,1:T(8,128)(2,1)S(1)} %slice.99), channel_id=1, source_target_pairs={{0,8},{1,9},{2,10},{3,11},{4,12},{5,13},{6,14},{7,15},{16,24},{17,... | collective-permute-start | bytes 2359304 | tf_op jit(solution)/shard_map/ppermute | solution.py:17
  25.0 23.9 %copy-start.2 = (s32[128]{0:T(128)S(1)}, s32[128]{0:T(128)}, u32[]{:S(2)}) copy-start(s32[128]{0:T(128)} %param.5) | copy-start | bytes 1540
  78.9 99.5 %all-to-all-start = ((bf16[128,64,2,128]{3,2,1,0:T(2,128)(2,1)}), bf16[128,64,2,128]{3,2,1,0:T(2,128)(2,1)}, u32[]{:S(2)}, u32[]{:S(2)}) async-start(bf16[128,64,2,128]{3,2,1,0:T(2,128)(2,1)} %copy.19), calls=%async_computation | async-start | bytes 8388608 | tf_op jit(solution)/shard_map/all_to_all | solution.py:91
  181.8 2.0 copy-start
  220.5 6.7 %copy-start.1 = (bf16[16,128,512,1]{2,1,0,3:T(8,128)(2,1)S(1)}, bf16[16,128,512,1]{2,1,0,3:T(8,128)(2,1)}, u32[]{:S(2)}) copy-start(bf16[16,128,512,1]{2,1,0,3:T(8,128)(2,1)} %reshape.177) | copy-start | bytes 6291460
Sparse Core Ops, SparseCore 0:
  54.5 15.7 all-gather.1
where the time goes:
time: 253 us
  waiting for transfers between devices  110 us (43%)
  local copies, waits for them, and re-layouts  55.4 us (22%)
  matrix products  44.1 us (17%)
  other arithmetic  21.6 us (9%)
  between operations  13.5 us (5%)
  starting transfers between devices  8.18 us (3%)
    all_to_all x1, waiting for transfers between devices, local(): lax.all_to_all(timed, 'inp', split_axis=0, concat_axis=3, tiled=True)  93.7 us
    dot_general x2, matrix products, transform(): jnp.dot(filtered.reshape(rows * frames, width), table, precision=lax.Prec...  25.7 us
    another operation x3, local copies, waits for them, and re-layouts, correlate(): left_both = jnp.stack([real_rows, imag_rows], axis=1)  20.5 us
    dot_general x1, matrix products, correlate(): jnp.einsum('crka,ckb->crab', left_both, right_rows, preferred_element_typ...  18.4 us
    all_gather x1, waiting for transfers between devices, local(): timed = lax.all_gather(channels, 'tm', axis=1, tiled=True)  15.9 us
    all_to_all x3, local copies, waits for them, and re-layouts, local(): lax.all_to_all(timed, 'inp', split_axis=0, concat_axis=3, tiled=True)  12.3 us
    all_gather x1, local copies, waits for them, and re-layouts, local(): timed = lax.all_gather(channels, 'tm', axis=1, tiled=True)  8.51 us
    reshape x1, other arithmetic, local(): voltage = (samples.astype(jnp.float32) / 128.0).astype(jnp.bfloat16).resh...  7.14 us
  transfers between devices with their start and end apart: 3, of which 2 were waited for; matrix products, arithmetic and copies ran while one was open for 10% of the time, Pallas kernels for 0%

commit v1 on v0

v1 whole, which is shorter than its diff:
```python
import functools
import math

import jax
import jax.numpy as jnp
import ml_dtypes
import numpy as np
from jax import lax
from jax.experimental import pallas as pl
from jax.experimental.pallas import tpu as pltpu
from jax.sharding import PartitionSpec as P

NFFT = 1024
TAPS = 4
CH_FIRST = 384
CH = 128
LANES = 128
STEP = 4
HALF = 16
VMEM = 56 * 2**20


def window_values():
    positions = np.arange(TAPS * NFFT, dtype=np.float64) + 0.5
    shaped = np.sinc((positions - TAPS * NFFT / 2) / NFFT)
    taper = 0.5 - 0.5 * np.cos(2 * math.pi * positions / (TAPS * NFFT))
    return (shaped * taper).reshape(TAPS, NFFT)


def transform_values():
    sample_idx = np.arange(NFFT)
    chan_idx = CH_FIRST + np.arange(CH)
    angles = (sample_idx[:, None] * chan_idx[None, :] % NFFT) * (2 * math.pi / NFFT)
    both = np.concatenate([np.cos(angles), -np.sin(angles)], axis=1)
    return both / math.sqrt(NFFT)


def split_table():
    table = transform_values()
    high = table.astype(ml_dtypes.bfloat16)
    low = (table - high.astype(np.float64)).astype(ml_dtypes.bfloat16)
    return high, low


def ring(length, by):
    return [(i, (i + by) % length) for i in range(length)]


def channelize_kernel(n, cuts, me_ref, flags_ref, window_ref, high_ref, low_ref, prev_ref,
                      samples_ref, *rest):
    outs, (carry, filt_high, filt_low, spectra) = rest[:-4], rest[-4:]
    step = pl.program_id(0)
    rows = samples_ref.shape[0]

    @pl.when(step == 0)
    def _():
        carry[...] = prev_ref[:, NFFT:].astype(jnp.float32)

    width = 256
    for lane in range(0, NFFT, width):
        taps = [window_ref[k : k + 1, lane : lane + width] for k in range(TAPS)]

        def strip(r, _):
            at = pl.ds(pl.multiple_of(r * 16, 16), 16)
            held = [carry[at, j * NFFT + lane : j * NFFT + lane + width] for j in range(TAPS - 1)]
            for f in range(STEP):
                value = samples_ref[at, f * NFFT + lane : f * NFFT + lane + width]
                held.append(value.astype(jnp.float32))
                total = taps[0] * held[-1]
                for k in range(1, TAPS):
                    total = total + taps[k] * held[-1 - k]
                high = total.astype(jnp.bfloat16)
                low = (total - high.astype(jnp.float32)).astype(jnp.bfloat16)
                to = pl.ds(pl.multiple_of(f * rows + r * 16, 16), 16)
                filt_high[to, lane : lane + width] = high
                filt_low[to, lane : lane + width] = low
                held = held[1:]
            for j in range(TAPS - 1):
                carry[at, j * NFFT + lane : j * NFFT + lane + width] = held[j]
            return 0

        lax.fori_loop(0, rows // 16, strip, 0)

    dot = functools.partial(jnp.dot, preferred_element_type=jnp.float32)
    for f in range(STEP):
        at = slice(f * rows, (f + 1) * rows)
        high = filt_high[at, :]
        out = dot(high, high_ref[...]) + dot(filt_low[at, :], high_ref[...]) + dot(high, low_ref[...])
        for p in range(2):
            part = out[:, p * CH : (p + 1) * CH].T * flags_ref[...]
            row = (p * HALF + step * STEP + f) * CH
            spectra[pl.ds(pl.multiple_of(row, CH), CH), :] = part

    @pl.when(step == pl.num_programs(0) - 1)
    def _():
        per = CH // n
        for d in range(n):
            first = lax.rem(me_ref[0] + d, n) * per
            begin = 0
            for g, count in enumerate(cuts):
                for c in range(count):
                    picked = spectra[pl.ds(first + begin + c, 2 * HALF, stride=CH), :]
                    outs[g * n + d][c] = picked.astype(jnp.bfloat16)
                begin += count


def channelize(me, samples, prev, prev_block, first_step, flags, n, cuts):
    rows = samples.shape[0]
    high, low = split_table()
    whole = lambda *shape: pl.BlockSpec(shape, lambda i, me: (0,) * len(shape))
    shapes = [(count, 2 * HALF, rows) for count in cuts for _ in range(n)]
    steps = HALF // STEP
    out = pl.pallas_call(
        functools.partial(channelize_kernel, n, cuts),
        grid_spec=pltpu.PrefetchScalarGridSpec(
            num_scalar_prefetch=1,
            grid=(steps,),
            in_specs=[
                whole(1, rows),
                whole(TAPS, NFFT),
                whole(NFFT, 2 * CH),
                whole(NFFT, 2 * CH),
                pl.BlockSpec((rows, TAPS * NFFT), lambda i, me: (0, prev_block)),
                pl.BlockSpec((rows, STEP * NFFT), lambda i, me: (0, first_step + i)),
            ],
            out_specs=[whole(*shape) for shape in shapes],
            scratch_shapes=[
                pltpu.VMEM((rows, (TAPS - 1) * NFFT), jnp.float32),
                pltpu.VMEM((STEP * rows, NFFT), jnp.bfloat16),
                pltpu.VMEM((STEP * rows, NFFT), jnp.bfloat16),
                pltpu.VMEM((2 * HALF * CH, LANES), jnp.float32),
            ],
        ),
        out_shape=[jax.ShapeDtypeStruct(shape, jnp.bfloat16) for shape in shapes],
        compiler_params=pltpu.CompilerParams(vmem_limit_bytes=VMEM),
        cost_estimate=pl.CostEstimate(
            flops=6 * 2 * rows * HALF * NFFT * 2 * CH,
            bytes_accessed=rows * (HALF + TAPS) * NFFT * 4,
            transcendentals=0,
        ),
        name="channelize",
    )(me, flags, jnp.asarray(window_values() / 128, jnp.float32), jnp.asarray(high),
      jnp.asarray(low), prev, samples)
    return [out[g * n : (g + 1) * n] for g in range(len(cuts))]


def correlate_kernel(n, tiles, place_ref, *rest):
    blocks, (out_ref, left, turned) = rest[:4], rest[-3:]
    me, half = place_ref[0], place_ref[1]
    for d in range(n):
        src = lax.rem(me + (n - d), n)
        for b, block in enumerate(blocks):
            real = block[d, 0, :HALF, :]
            imag = block[d, 0, HALF:, :]
            low = slice(b * HALF, (b + 1) * HALF)
            high = slice((4 + b) * HALF, (5 + b) * HALF)
            left[src, low, :] = real
            left[src, high, :] = imag
            turned[src, low, :] = imag
            turned[src, high, :] = -real
    right = jnp.concatenate([left[half * tiles + j] for j in range(tiles)], axis=1)
    dims = (((0,), (0,)), ((), ()))

    def product(s, _):
        to = pl.ds(pl.multiple_of(s * LANES, LANES), LANES)
        for part, source in enumerate((left, turned)):
            out = lax.dot_general(source[s], right, dims, preferred_element_type=jnp.float32)
            out_ref[0, part, to, :] = out.astype(jnp.bfloat16)
        return 0

    lax.fori_loop(0, n, product, 0)


def correlate(place, blocks, offsets, first, count, per, width, before):
    n = blocks[0].shape[0]
    rows = blocks[0].shape[3]
    in_specs = [
        pl.BlockSpec((n, 1, 2 * HALF, rows), functools.partial(lambda o, i, place: (0, o + i, 0, 0), o))
        for o in offsets
    ]
    operands = list(blocks)
    aliases = {}
    if before is not None:
        in_specs.append(pl.BlockSpec(memory_space=pl.ANY))
        operands.append(before)
        aliases = {1 + 4: 0}
    shape = (per, 2, n * rows, width)
    return pl.pallas_call(
        functools.partial(correlate_kernel, n, width // rows),
        grid_spec=pltpu.PrefetchScalarGridSpec(
            num_scalar_prefetch=1,
            grid=(count,),
            in_specs=in_specs,
            out_specs=pl.BlockSpec((1,) + shape[1:], lambda i, place: (first + i, 0, 0, 0)),
            scratch_shapes=[pltpu.VMEM((n, 8 * HALF, rows), jnp.bfloat16)] * 2,
        ),
        out_shape=jax.ShapeDtypeStruct(shape, jnp.bfloat16),
        input_output_aliases=aliases,
        compiler_params=pltpu.CompilerParams(vmem_limit_bytes=VMEM),
        cost_estimate=pl.CostEstimate(
            flops=count * 2 * 2 * 8 * HALF * n * rows * width,
            bytes_accessed=count * 2 * n * rows * width * 2,
            transcendentals=0,
        ),
        name="correlate",
    )(place, *operands)


def exchanged(parts, order):
    n = len(parts)
    out = list(parts)
    for d in order:
        out[d] = lax.ppermute(parts[d], "inp", ring(n, d))
    return out


def tiled_local(samples, flags):
    n = lax.axis_size("inp")
    tm = lax.axis_size("tm")
    rows = samples.shape[0]
    per = CH // n
    me = lax.axis_index("inp").astype(jnp.int32)
    half = lax.axis_index("tm").astype(jnp.int32)
    weight = flags.astype(jnp.float32).reshape(1, rows)
    order = sorted(range(1, n), key=lambda d: abs(d - n / 2))
    cuts = (per - 6, 6)
    place = jnp.stack([me, half])

    (late,) = channelize(me.reshape(1), samples, samples, HALF // STEP - 1, HALF // STEP, weight, n, (per,))
    late_in = exchanged(late, order)
    tail = samples[:, samples.shape[1] - TAPS * NFFT :].astype(jnp.bfloat16)
    halo = lax.ppermute(tail, "tm", [(i, i + 1) for i in range(tm - 1)])
    early = channelize(me.reshape(1), samples, halo, 0, 0, weight, n, cuts)
    swap = [(i, tm - 1 - i) for i in range(tm)]
    late_own = jnp.stack(late_in)
    late_other = lax.ppermute(late_own, "tm", swap)
    result, first = None, 0
    for part, count in zip(early, cuts):
        own = jnp.stack(exchanged(part, order))
        other = lax.ppermute(own, "tm", swap)
        result = correlate(place, (late_own, late_other, own, other), (first, first, 0, 0), first,
                           count, per, n * rows // tm, result)
        first += count
    return result


def filter_bank(extended, window, frames):
    return sum(
        window[k] * extended[:, TAPS - 1 - k : TAPS - 1 - k + frames] for k in range(TAPS)
    )


def plain_local(samples, flags):
    rows = samples.shape[0]
    frames = samples.shape[1] // NFFT
    window = jnp.asarray(window_values(), jnp.float32)
    table = jnp.asarray(transform_values(), jnp.float32)
    voltage = (samples.astype(jnp.float32) / 128.0).reshape(rows, frames, NFFT)
    length = lax.axis_size("tm")
    tail = voltage[:, frames - (TAPS - 1) :].astype(jnp.bfloat16)
    halo = lax.ppermute(tail, "tm", [(i, i + 1) for i in range(length - 1)])
    extended = jnp.concatenate([halo.astype(jnp.float32), voltage], axis=1)
    filtered = filter_bank(extended, window, frames)
    spectra = jnp.dot(
        filtered.reshape(rows * frames, NFFT),
        table,
        precision=lax.Precision.HIGHEST,
        preferred_element_type=jnp.float32,
    ).reshape(rows, frames, 2, CH)
    weight = flags.astype(jnp.float32)[:, None, None, None]
    channels = (spectra * weight).astype(jnp.bfloat16).transpose(3, 1, 2, 0)
    mine = lax.all_to_all(channels, "inp", split_axis=0, concat_axis=3, tiled=True)
    left = lax.all_gather(mine, "tm", axis=1, tiled=True)
    chans, total_frames, _, total = left.shape
    width = total // length
    depth = 2 * total_frames
    turned = jnp.stack([left[:, :, 1], -left[:, :, 0]], axis=2).reshape(chans, depth, total)
    straight = left.reshape(chans, depth, total)
    right = lax.dynamic_slice_in_dim(straight, lax.axis_index("tm") * width, width, 2)
    both = jnp.stack([straight, turned], axis=1)
    out = jnp.einsum("crka,ckb->crab", both, right, preferred_element_type=jnp.float32)
    return out.astype(jnp.bfloat16)


def local(samples, flags):
    n, tm = lax.axis_size("inp"), lax.axis_size("tm")
    rows, frames = samples.shape[0], samples.shape[1] // NFFT
    fits = rows == LANES and frames == 2 * HALF and tm == 2 and n % tm == 0 and CH // n > 8
    return tiled_local(samples, flags) if fits else plain_local(samples, flags)


def solution(mesh):
    return jax.shard_map(
        local,
        mesh=mesh,
        in_specs=(P("inp", ("band", "tm")), P(("band", "inp"))),
        out_specs=P(("band", "inp"), None, None, "tm"),
        check_vma=False,
    )
```

time: 253 us -> 162 us (0.64)
  waiting for transfers between devices: 110 us -> 41.4 us
  Pallas kernels: 0 us -> 66.3 us
  local copies, waits for them, and re-layouts: 55.4 us -> 10.7 us
  matrix products: 44.1 us -> 0 us
  starting transfers between devices: 8.18 us -> 39.4 us
  other arithmetic: 21.6 us -> 3.45 us
  between operations: 13.5 us -> 0.2 us
    all_to_all x1 -> x0, waiting for transfers between devices: 93.7 us -> none  [local(): lax.all_to_all(timed, 'inp', split_axis=0, concat_axis=3, tiled=True)]
    pallas_call x0 -> x4, Pallas kernels: none -> 66.3 us  [the longest x2 40 us: correlate(): pl.pallas_call(functools.partial(correlate_kernel, n, width // rows), gri...]
    dot_general x3 -> x0, matrix products: 44.1 us -> none  [the longest x2 25.7 us: transform(): jnp.dot(filtered.reshape(rows * frames, width), table, precision=lax.Prec...]
    ppermute x1 -> x25, waiting for transfers between devices: 0.01 us -> 41.4 us  [the longest x21 41 us: exchanged(): out[d] = lax.ppermute(parts[d], 'inp', ring(n, d))]
    ppermute x1 -> x25, starting transfers between devices: 2.41 us -> 39.4 us  [the longest x21 37.1 us: exchanged(): out[d] = lax.ppermute(parts[d], 'inp', ring(n, d))]
    another operation x4 -> x3, local copies, waits for them, and re-layouts: 24.9 us -> 0.65 us  [the longest x2 0.63 us: tiled_local(): own = jnp.stack(exchanged(part, order))]
    all_gather x1 -> x0, waiting for transfers between devices: 15.9 us -> none  [local(): timed = lax.all_gather(channels, 'tm', axis=1, tiled=True)]
    all_to_all x3 -> x0, local copies, waits for them, and re-layouts: 12.3 us -> none  [local(): lax.all_to_all(timed, 'inp', split_axis=0, concat_axis=3, tiled=True)]
  transfers between devices with their start and end apart: 3 -> 25, of which waited for: 2 -> 10; matrix products, arithmetic and copies ran while one was open for 10% -> 6% of each run, Pallas kernels for 0% -> 23%
where the time goes in v1:
time: 162 us; the launch traced here: 161 us
  Pallas kernels  66.3 us (41%)
  waiting for transfers between devices  41.4 us (26%)
  starting transfers between devices  39.4 us (24%)
  local copies, waits for them, and re-layouts  10.7 us (7%)
  other arithmetic  3.45 us (2%)
    ppermute x21, waiting for transfers between devices, exchanged(): out[d] = lax.ppermute(parts[d], 'inp', ring(n, d))  41 us
    pallas_call x2, Pallas kernels, correlate(): pl.pallas_call(functools.partial(correlate_kernel, n, width // rows), gri...  40 us
    ppermute x21, starting transfers between devices, exchanged(): out[d] = lax.ppermute(parts[d], 'inp', ring(n, d))  37.1 us
    pallas_call x2, Pallas kernels, channelize(): pl.pallas_call(functools.partial(channelize_kernel, n, cuts), grid_spec=p...  26.3 us
    unnamed x31, local copies, waits for them, and re-layouts  10 us
  transfers between devices with their start and end apart: 25, of which 10 were waited for; matrix products, arithmetic and copies ran while one was open for 6% of the time, Pallas kernels for 23%

profile of v1, /device:TPU:0, one launch (start us, length us, event | category | flops | bytes accessed | tf_op | source)
XLA Modules:
  0.0 161.4 jit_solution(4188880330609448229)
XLA Ops:
  0.0 1.2 convert_bitcast_fusion.flags_ref
  1.2 13.3 %channelize.2 = (bf16[16,32,128]{2,1,0:T(8,128)(2,1)}, bf16[16,32,128]{2,1,0:T(8,128)(2,1)}, bf16[16,32,128]{2,1,0:T(8,128)(2,1)}, bf16[16,32,128]{2,1,0:T(8,128...) custom-call(s32[1]{0:T(128)} %bitcast.me_ref, ...), custom_call_target="tpu_custom_call" | custom-call | flops 6442450944 | bytes 10485760 | tf_op jit(solution)/shard_map/channelize/pallas_call | solution.py:113
  14.4 3.0 %collective-permute-start = (bf16[16,32,128]{2,1,0:T(8,128)(2,1)}, bf16[16,32,128]{2,1,0:T(8,128)(2,1)S(1)}, u32[]{:S(2)}, u32[]{:S(2)}) collective-permute-start(bf16[16,32,128]{2,1,0:T(8,128)(2,1)} %get-tuple-element.30), channel_id=1, source_target_pairs={{0,1},{1,2},{2,3},{3,4},{4,5},{5,6},{6,7},{7,0},{8,9},{9,10},{10,1... | collective-permute-start | bytes 393224 | tf_op jit(solution)/shard_map/ppermute | solution.py:213
  17.4 1.6 collective-permute-start.1
  19.0 2.5 %collective-permute-start.2 = (bf16[16,32,128]{2,1,0:T(8,128)(2,1)}, bf16[16,32,128]{2,1,0:T(8,128)(2,1)S(1)}, u32[]{:S(2)}, u32[]{:S(2)}) collective-permute-start(bf16[16,32,128]{2,1,0:T(8,128)(2,1)} %get-tuple-element.32), channel_id=1, source_target_pairs={{0,3},{1,4},{2,5},{3,6},{4,7},{5,0},{6,1},{7,2},{8,11},{9,12},{10,... | collective-permute-start | bytes 393224 | tf_op jit(solution)/shard_map/ppermute | solution.py:213
  21.5 1.2 collective-permute-start.3
  22.8 2.6 %collective-permute-start.4 = (bf16[16,32,128]{2,1,0:T(8,128)(2,1)}, bf16[16,32,128]{2,1,0:T(8,128)(2,1)S(1)}, u32[]{:S(2)}, u32[]{:S(2)}) collective-permute-start(bf16[16,32,128]{2,1,0:T(8,128)(2,1)} %get-tuple-element.34), channel_id=1, source_target_pairs={{0,5},{1,6},{2,7},{3,0},{4,1},{5,2},{6,3},{7,4},{8,13},{9,14},{10,... | collective-permute-start | bytes 393224 | tf_op jit(solution)/shard_map/ppermute | solution.py:213
  25.4 1.7 %slice_convert_fusion = bf16[128,4096]{1,0:T(8,128)(2,1)S(1)} fusion(s32[128,32768]{1,0:T(8,128)} %samples_ref.3), kind=kLoop, calls=%fused_computation | loop fusion | flops 524288 | bytes 3145728 | tf_op jit(solution)/shard_map/convert
  28.1 1.4 collective-permute-start.5
  29.5 1.5 collective-permute-start.6
  31.0 4.6 %collective-permute-done.2 = bf16[16,32,128]{2,1,0:T(8,128)(2,1)S(1)} collective-permute-done((bf16[16,32,128]{2,1,0:T(8,128)(2,1)}, bf16[16,32,128]{2,1,0:T(8,128)(2,1)S(1)}, u32[]{:S(2)}, u32[]{:S(2)}) %collective-permute-start.2) | collective-permute-done | bytes 131104 | tf_op jit(solution)/shard_map/ppermute | solution.py:213
  35.6 1.8 %collective-permute-start.8 = (bf16[128,4096]{1,0:T(8,128)(2,1)S(1)}, bf16[128,4096]{1,0:T(8,128)(2,1)S(1)}, u32[]{:S(2)}, u32[]{:S(2)}) collective-permute-start(bf16[128,4096]{1,0:T(8,128)(2,1)S(1)} %slice_convert_fusion), channel_id=1, source_target_pairs={{0,8},{1,9},{2,10},{3,11},{4,12},{5,13},{6,14},{7,15},{16,24},{17,... | collective-permute-start | bytes 3145736 | tf_op jit(solution)/shard_map/ppermute | solution.py:232
  37.5 1.6 collective-permute-done.5
  40.6 13.0 %channelize.3 = (bf16[10,32,128]{2,1,0:T(8,128)(2,1)}, bf16[10,32,128]{2,1,0:T(8,128)(2,1)}, bf16[10,32,128]{2,1,0:T(8,128)(2,1)}, bf16[10,32,128]{2,1,0:T(8,128...) custom-call(s32[1]{0:T(128)} %bitcast.me_ref, ...), custom_call_target="tpu_custom_call" | custom-call | flops 6442450944 | bytes 10485760 | tf_op jit(solution)/shard_map/channelize/pallas_call | solution.py:113
  53.6 2.6 %collective-permute-start.9 = (bf16[6,32,128]{2,1,0:T(8,128)(2,1)}, bf16[6,32,128]{2,1,0:T(8,128)(2,1)S(1)}, u32[]{:S(2)}, u32[]{:S(2)}) collective-permute-start(bf16[6,32,128]{2,1,0:T(8,128)(2,1)} %get-tuple-element.38), channel_id=1, source_target_pairs={{0,1},{1,2},{2,3},{3,4},{4,5},{5,6},{6,7},{7,0},{8,9},{9,10},{10,1... | collective-permute-start | bytes 147464 | tf_op jit(solution)/shard_map/ppermute | solution.py:213
  56.2 4.2 %collective-permute-start.10 = (bf16[6,32,128]{2,1,0:T(8,128)(2,1)}, bf16[6,32,128]{2,1,0:T(8,128)(2,1)S(1)}, u32[]{:S(2)}, u32[]{:S(2)}) collective-permute-start(bf16[6,32,128]{2,1,0:T(8,128)(2,1)} %get-tuple-element.39), channel_id=1, source_target_pairs={{0,2},{1,3},{2,4},{3,5},{4,6},{5,7},{6,0},{7,1},{8,10},{9,11},{10,... | collective-permute-start | bytes 147464 | tf_op jit(solution)/shard_map/ppermute | solution.py:213
  60.4 2.9 %collective-permute-start.11 = (bf16[6,32,128]{2,1,0:T(8,128)(2,1)}, bf16[6,32,128]{2,1,0:T(8,128)(2,1)S(1)}, u32[]{:S(2)}, u32[]{:S(2)}) collective-permute-start(bf16[6,32,128]{2,1,0:T(8,128)(2,1)} %get-tuple-element.40), channel_id=1, source_target_pairs={{0,3},{1,4},{2,5},{3,6},{4,7},{5,0},{6,1},{7,2},{8,11},{9,12},{10,... | collective-permute-start | bytes 147464 | tf_op jit(solution)/shard_map/ppermute | solution.py:213
  64.2 1.4 constant_dynamic-update-slice_fusion.7
  65.6 2.5 %collective-permute-start.13 = (bf16[6,32,128]{2,1,0:T(8,128)(2,1)}, bf16[6,32,128]{2,1,0:T(8,128)(2,1)S(1)}, u32[]{:S(2)}, u32[]{:S(2)}) collective-permute-start(bf16[6,32,128]{2,1,0:T(8,128)(2,1)} %get-tuple-element.42), channel_id=1, source_target_pairs={{0,5},{1,6},{2,7},{3,0},{4,1},{5,2},{6,3},{7,4},{8,13},{9,14},{10,... | collective-permute-start | bytes 147464 | tf_op jit(solution)/shard_map/ppermute | solution.py:213
  68.8 1.8 %collective-permute-start.14 = (bf16[6,32,128]{2,1,0:T(8,128)(2,1)}, bf16[6,32,128]{2,1,0:T(8,128)(2,1)S(1)}, u32[]{:S(2)}, u32[]{:S(2)}) collective-permute-start(bf16[6,32,128]{2,1,0:T(8,128)(2,1)} %get-tuple-element.43), channel_id=1, source_target_pairs={{0,6},{1,7},{2,0},{3,1},{4,2},{5,3},{6,4},{7,5},{8,14},{9,15},{10,... | collective-permute-start | bytes 147464 | tf_op jit(solution)/shard_map/ppermute | solution.py:213
  72.8 1.0 collective-permute-start.17
  74.4 5.7 %collective-permute-done.17 = bf16[10,32,128]{2,1,0:T(8,128)(2,1)S(1)} collective-permute-done((bf16[10,32,128]{2,1,0:T(8,128)(2,1)}, bf16[10,32,128]{2,1,0:T(8,128)(2,1)S(1)}, u32[]{:S(2)}, u32[]{:S(2)}) %collective-permute-start.17) | collective-permute-done | bytes 81952 | tf_op jit(solution)/shard_map/ppermute | solution.py:213
  81.0 6.4 %collective-permute-done.18 = bf16[10,32,128]{2,1,0:T(8,128)(2,1)S(1)} collective-permute-done((bf16[10,32,128]{2,1,0:T(8,128)(2,1)}, bf16[10,32,128]{2,1,0:T(8,128)(2,1)S(1)}, u32[]{:S(2)}, u32[]{:S(2)}) %collective-permute-start.18) | collective-permute-done | bytes 81952 | tf_op jit(solution)/shard_map/ppermute | solution.py:213
  87.4 6.7 %collective-permute-done.19 = bf16[10,32,128]{2,1,0:T(8,128)(2,1)S(1)} collective-permute-done((bf16[10,32,128]{2,1,0:T(8,128)(2,1)}, bf16[10,32,128]{2,1,0:T(8,128)(2,1)S(1)}, u32[]{:S(2)}, u32[]{:S(2)}) %collective-permute-start.19) | collective-permute-done | bytes 81952 | tf_op jit(solution)/shard_map/ppermute | solution.py:213
  94.2 5.6 %collective-permute-done.20 = bf16[10,32,128]{2,1,0:T(8,128)(2,1)S(1)} collective-permute-done((bf16[10,32,128]{2,1,0:T(8,128)(2,1)}, bf16[10,32,128]{2,1,0:T(8,128)(2,1)S(1)}, u32[]{:S(2)}, u32[]{:S(2)}) %collective-permute-start.20) | collective-permute-done | bytes 81952 | tf_op jit(solution)/shard_map/ppermute | solution.py:213
  99.8 5.6 %collective-permute-done.21 = bf16[10,32,128]{2,1,0:T(8,128)(2,1)S(1)} collective-permute-done((bf16[10,32,128]{2,1,0:T(8,128)(2,1)}, bf16[10,32,128]{2,1,0:T(8,128)(2,1)S(1)}, u32[]{:S(2)}, u32[]{:S(2)}) %collective-permute-start.21) | collective-permute-done | bytes 81952 | tf_op jit(solution)/shard_map/ppermute | solution.py:213
  105.4 3.3 %collective-permute-start.22 = (bf16[10,32,128]{2,1,0:T(8,128)(2,1)}, bf16[10,32,128]{2,1,0:T(8,128)(2,1)S(1)}, u32[]{:S(2)}, u32[]{:S(2)}) collective-permute-start(bf16[10,32,128]{2,1,0:T(8,128)(2,1)} %get-tuple-element.51), channel_id=1, source_target_pairs={{0,6},{1,7},{2,0},{3,1},{4,2},{5,3},{6,4},{7,5},{8,14},{9,15},{10,... | collective-permute-start | bytes 245768 | tf_op jit(solution)/shard_map/ppermute | solution.py:213
  108.7 2.4 %collective-permute-done.22 = bf16[10,32,128]{2,1,0:T(8,128)(2,1)S(1)} collective-permute-done((bf16[10,32,128]{2,1,0:T(8,128)(2,1)}, bf16[10,32,128]{2,1,0:T(8,128)(2,1)S(1)}, u32[]{:S(2)}, u32[]{:S(2)}) %collective-permute-start.22) | collective-permute-done | bytes 81952 | tf_op jit(solution)/shard_map/ppermute | solution.py:213
  111.1 3.1 %collective-permute-start.23 = (bf16[10,32,128]{2,1,0:T(8,128)(2,1)}, bf16[10,32,128]{2,1,0:T(8,128)(2,1)S(1)}, u32[]{:S(2)}, u32[]{:S(2)}) collective-permute-start(bf16[10,32,128]{2,1,0:T(8,128)(2,1)} %get-tuple-element.52), channel_id=1, source_target_pairs={{0,7},{1,0},{2,1},{3,2},{4,3},{5,4},{6,5},{7,6},{8,15},{9,8},{10,9... | collective-permute-start | bytes 245768 | tf_op jit(solution)/shard_map/ppermute | solution.py:213
  114.2 2.4 %collective-permute-done.23 = bf16[10,32,128]{2,1,0:T(8,128)(2,1)S(1)} collective-permute-done((bf16[10,32,128]{2,1,0:T(8,128)(2,1)}, bf16[10,32,128]{2,1,0:T(8,128)(2,1)S(1)}, u32[]{:S(2)}, u32[]{:S(2)}) %collective-permute-start.23) | collective-permute-done | bytes 81952 | tf_op jit(solution)/shard_map/ppermute | solution.py:213
  121.4 24.3 %correlate.2.rest_4_ = bf16[16,2,1024,512]{3,2,1,0:T(8,128)(2,1)} custom-call(s32[2]{0:T(128)} %pad_add_fusion.place_ref, bf16[8,16,32,128]{3,2,1,0:T(8,128)(2,1)} %copy-done, bf16[8,16,32,128]{3,2,1,0:T(8,128)(2,1)} %copy-done.1, bf16[8,10,32,128]{3,2,1,0:T(8,128)(2,1)} %copy-done.2, bf16[8,10,32,128]{3,2,1,0:T(8,128)(2,1)} %copy-done.3), custom_call_target="tpu_custom_call" | custom-call | flops 2684354560 | bytes 20971520 | tf_op jit(solution)/shard_map/correlate/pallas_call | solution.py:188
  145.7 15.8 %correlate.3 = bf16[16,2,1024,512]{3,2,1,0:T(8,128)(2,1)} custom-call(s32[2]{0:T(128)} %pad_add_fusion.place_ref, bf16[8,16,32,128]{3,2,1,0:T(8,128)(2,1)} %copy-done, bf16[8,16,32,128]{3,2,1,0:T(8,128)(2,1)} %copy-done.1, bf16[8,6,32,128]{3,2,1,0:T(8,128)(2,1)} %constant_dynamic-update-slice_fusion.rest_2_, ...), custom_call_target="tpu_custom_call", output_to_operand_aliasing={{}: (5, {})} | custom-call | flops 1610612736 | bytes 12582912 | tf_op jit(solution)/shard_map/correlate/pallas_call | solution.py:188
  (59 shorter events, 12.6 us)
Async XLA Ops:
  14.4 13.6 %collective-permute-start = (bf16[16,32,128]{2,1,0:T(8,128)(2,1)}, bf16[16,32,128]{2,1,0:T(8,128)(2,1)S(1)}, u32[]{:S(2)}, u32[]{:S(2)}) collective-permute-start(bf16[16,32,128]{2,1,0:T(8,128)(2,1)} %get-tuple-element.30), channel_id=1, source_target_pairs={{0,1},{1,2},{2,3},{3,4},{4,5},{5,6},{6,7},{7,0},{8,9},{9,10},{10,1... | collective-permute-start | bytes 393224 | tf_op jit(solution)/shard_map/ppermute | solution.py:213
  17.4 12.1 %collective-permute-start.1 = (bf16[16,32,128]{2,1,0:T(8,128)(2,1)}, bf16[16,32,128]{2,1,0:T(8,128)(2,1)S(1)}, u32[]{:S(2)}, u32[]{:S(2)}) collective-permute-start(bf16[16,32,128]{2,1,0:T(8,128)(2,1)} %get-tuple-element.31), channel_id=1, source_target_pairs={{0,2},{1,3},{2,4},{3,5},{4,6},{5,7},{6,0},{7,1},{8,10},{9,11},{10,... | collective-permute-start | bytes 393224 | tf_op jit(solution)/shard_map/ppermute | solution.py:213
  19.0 16.6 %collective-permute-start.2 = (bf16[16,32,128]{2,1,0:T(8,128)(2,1)}, bf16[16,32,128]{2,1,0:T(8,128)(2,1)S(1)}, u32[]{:S(2)}, u32[]{:S(2)}) collective-permute-start(bf16[16,32,128]{2,1,0:T(8,128)(2,1)} %get-tuple-element.32), channel_id=1, source_target_pairs={{0,3},{1,4},{2,5},{3,6},{4,7},{5,0},{6,1},{7,2},{8,11},{9,12},{10,... | collective-permute-start | bytes 393224 | tf_op jit(solution)/shard_map/ppermute | solution.py:213
  21.5 15.9 %collective-permute-start.3 = (bf16[16,32,128]{2,1,0:T(8,128)(2,1)}, bf16[16,32,128]{2,1,0:T(8,128)(2,1)S(1)}, u32[]{:S(2)}, u32[]{:S(2)}) collective-permute-start(bf16[16,32,128]{2,1,0:T(8,128)(2,1)} %get-tuple-element.33), channel_id=1, source_target_pairs={{0,4},{1,5},{2,6},{3,7},{4,0},{5,1},{6,2},{7,3},{8,12},{9,13},{10,... | collective-permute-start | bytes 393224 | tf_op jit(solution)/shard_map/ppermute | solution.py:213
  22.8 14.7 %collective-permute-start.4 = (bf16[16,32,128]{2,1,0:T(8,128)(2,1)}, bf16[16,32,128]{2,1,0:T(8,128)(2,1)S(1)}, u32[]{:S(2)}, u32[]{:S(2)}) collective-permute-start(bf16[16,32,128]{2,1,0:T(8,128)(2,1)} %get-tuple-element.34), channel_id=1, source_target_pairs={{0,5},{1,6},{2,7},{3,0},{4,1},{5,2},{6,3},{7,4},{8,13},{9,14},{10,... | collective-permute-start | bytes 393224 | tf_op jit(solution)/shard_map/ppermute | solution.py:213
  28.1 11.0 %collective-permute-start.5 = (bf16[16,32,128]{2,1,0:T(8,128)(2,1)}, bf16[16,32,128]{2,1,0:T(8,128)(2,1)S(1)}, u32[]{:S(2)}, u32[]{:S(2)}) collective-permute-start(bf16[16,32,128]{2,1,0:T(8,128)(2,1)} %get-tuple-element.35), channel_id=1, source_target_pairs={{0,6},{1,7},{2,0},{3,1},{4,2},{5,3},{6,4},{7,5},{8,14},{9,15},{10,... | collective-permute-start | bytes 393224 | tf_op jit(solution)/shard_map/ppermute | solution.py:213
  29.5 9.6 %collective-permute-start.6 = (bf16[16,32,128]{2,1,0:T(8,128)(2,1)}, bf16[16,32,128]{2,1,0:T(8,128)(2,1)S(1)}, u32[]{:S(2)}, u32[]{:S(2)}) collective-permute-start(bf16[16,32,128]{2,1,0:T(8,128)(2,1)} %get-tuple-element.36), channel_id=1, source_target_pairs={{0,7},{1,0},{2,1},{3,2},{4,3},{5,4},{6,5},{7,6},{8,15},{9,8},{10,9... | collective-permute-start | bytes 393224 | tf_op jit(solution)/shard_map/ppermute | solution.py:213
  35.6 4.0 %collective-permute-start.8 = (bf16[128,4096]{1,0:T(8,128)(2,1)S(1)}, bf16[128,4096]{1,0:T(8,128)(2,1)S(1)}, u32[]{:S(2)}, u32[]{:S(2)}) collective-permute-start(bf16[128,4096]{1,0:T(8,128)(2,1)S(1)} %slice_convert_fusion), channel_id=1, source_target_pairs={{0,8},{1,9},{2,10},{3,11},{4,12},{5,13},{6,14},{7,15},{16,24},{17,... | collective-permute-start | bytes 3145736 | tf_op jit(solution)/shard_map/ppermute | solution.py:232
  39.2 80.4 %copy-start = (bf16[8,16,32,128]{3,2,1,0:T(8,128)(2,1)}, bf16[8,16,32,128]{3,2,1,0:T(8,128)(2,1)S(1)}, u32[]{:S(2)}) copy-start(bf16[8,16,32,128]{3,2,1,0:T(8,128)(2,1)S(1)} %bitcast_dynamic-update-slice_fusion.rest_0_) | copy-start | bytes 3145732
  39.2 80.4 %collective-permute-start.7 = (bf16[8,16,32,128]{3,2,1,0:T(8,128)(2,1)S(1)}, bf16[8,16,32,128]{3,2,1,0:T(8,128)(2,1)S(1)}, u32[]{:S(2)}, u32[]{:S(2)}) collective-permute-start(bf16[8,16,32,128]{3,2,1,0:T(8,128)(2,1)S(1)} %bitcast_dynamic-update-slice_fusion.rest_0_), channel_id=1, source_target_pairs={{0,8},{8,0},{1,9},{9,1},{2,10},{10,2},{3,11},{11,3},{4,12},{12,4},... | collective-permute-start | bytes 3145736 | tf_op jit(solution)/shard_map/ppermute | solution.py:236
  39.6 1.0 copy-start.4
  53.6 12.1 %collective-permute-start.9 = (bf16[6,32,128]{2,1,0:T(8,128)(2,1)}, bf16[6,32,128]{2,1,0:T(8,128)(2,1)S(1)}, u32[]{:S(2)}, u32[]{:S(2)}) collective-permute-start(bf16[6,32,128]{2,1,0:T(8,128)(2,1)} %get-tuple-element.38), channel_id=1, source_target_pairs={{0,1},{1,2},{2,3},{3,4},{4,5},{5,6},{6,7},{7,0},{8,9},{9,10},{10,1... | collective-permute-start | bytes 147464 | tf_op jit(solution)/shard_map/ppermute | solution.py:213
  56.2 12.6 %collective-permute-start.10 = (bf16[6,32,128]{2,1,0:T(8,128)(2,1)}, bf16[6,32,128]{2,1,0:T(8,128)(2,1)S(1)}, u32[]{:S(2)}, u32[]{:S(2)}) collective-permute-start(bf16[6,32,128]{2,1,0:T(8,128)(2,1)} %get-tuple-element.39), channel_id=1, source_target_pairs={{0,2},{1,3},{2,4},{3,5},{4,6},{5,7},{6,0},{7,1},{8,10},{9,11},{10,... | collective-permute-start | bytes 147464 | tf_op jit(solution)/shard_map/ppermute | solution.py:213
  60.4 10.8 %collective-permute-start.11 = (bf16[6,32,128]{2,1,0:T(8,128)(2,1)}, bf16[6,32,128]{2,1,0:T(8,128)(2,1)S(1)}, u32[]{:S(2)}, u32[]{:S(2)}) collective-permute-start(bf16[6,32,128]{2,1,0:T(8,128)(2,1)} %get-tuple-element.40), channel_id=1, source_target_pairs={{0,3},{1,4},{2,5},{3,6},{4,7},{5,0},{6,1},{7,2},{8,11},{9,12},{10,... | collective-permute-start | bytes 147464 | tf_op jit(solution)/shard_map/ppermute | solution.py:213
  63.3 9.5 %collective-permute-start.12 = (bf16[6,32,128]{2,1,0:T(8,128)(2,1)}, bf16[6,32,128]{2,1,0:T(8,128)(2,1)S(1)}, u32[]{:S(2)}, u32[]{:S(2)}) collective-permute-start(bf16[6,32,128]{2,1,0:T(8,128)(2,1)} %get-tuple-element.41), channel_id=1, source_target_pairs={{0,4},{1,5},{2,6},{3,7},{4,0},{5,1},{6,2},{7,3},{8,12},{9,13},{10,... | collective-permute-start | bytes 147464 | tf_op jit(solution)/shard_map/ppermute | solution.py:213
  65.6 51.0 %collective-permute-start.13 = (bf16[6,32,128]{2,1,0:T(8,128)(2,1)}, bf16[6,32,128]{2,1,0:T(8,128)(2,1)S(1)}, u32[]{:S(2)}, u32[]{:S(2)}) collective-permute-start(bf16[6,32,128]{2,1,0:T(8,128)(2,1)} %get-tuple-element.42), channel_id=1, source_target_pairs={{0,5},{1,6},{2,7},{3,0},{4,1},{5,2},{6,3},{7,4},{8,13},{9,14},{10,... | collective-permute-start | bytes 147464 | tf_op jit(solution)/shard_map/ppermute | solution.py:213
  68.8 48.7 %collective-permute-start.14 = (bf16[6,32,128]{2,1,0:T(8,128)(2,1)}, bf16[6,32,128]{2,1,0:T(8,128)(2,1)S(1)}, u32[]{:S(2)}, u32[]{:S(2)}) collective-permute-start(bf16[6,32,128]{2,1,0:T(8,128)(2,1)} %get-tuple-element.43), channel_id=1, source_target_pairs={{0,6},{1,7},{2,0},{3,1},{4,2},{5,3},{6,4},{7,5},{8,14},{9,15},{10,... | collective-permute-start | bytes 147464 | tf_op jit(solution)/shard_map/ppermute | solution.py:213
  71.2 46.9 %collective-permute-start.15 = (bf16[6,32,128]{2,1,0:T(8,128)(2,1)}, bf16[6,32,128]{2,1,0:T(8,128)(2,1)S(1)}, u32[]{:S(2)}, u32[]{:S(2)}) collective-permute-start(bf16[6,32,128]{2,1,0:T(8,128)(2,1)} %get-tuple-element.44), channel_id=1, source_target_pairs={{0,7},{1,0},{2,1},{3,2},{4,3},{5,4},{6,5},{7,6},{8,15},{9,8},{10,9... | collective-permute-start | bytes 147464 | tf_op jit(solution)/shard_map/ppermute | solution.py:213
  72.8 7.3 %collective-permute-start.17 = (bf16[10,32,128]{2,1,0:T(8,128)(2,1)}, bf16[10,32,128]{2,1,0:T(8,128)(2,1)S(1)}, u32[]{:S(2)}, u32[]{:S(2)}) collective-permute-start(bf16[10,32,128]{2,1,0:T(8,128)(2,1)} %get-tuple-element.46), channel_id=1, source_target_pairs={{0,1},{1,2},{2,3},{3,4},{4,5},{5,6},{6,7},{7,0},{8,9},{9,10},{10,1... | collective-permute-start | bytes 245768 | tf_op jit(solution)/shard_map/ppermute | solution.py:213
  80.1 7.3 %collective-permute-start.18 = (bf16[10,32,128]{2,1,0:T(8,128)(2,1)}, bf16[10,32,128]{2,1,0:T(8,128)(2,1)S(1)}, u32[]{:S(2)}, u32[]{:S(2)}) collective-permute-start(bf16[10,32,128]{2,1,0:T(8,128)(2,1)} %get-tuple-element.47), channel_id=1, source_target_pairs={{0,2},{1,3},{2,4},{3,5},{4,6},{5,7},{6,0},{7,1},{8,10},{9,11},{10,... | collective-permute-start | bytes 245768 | tf_op jit(solution)/shard_map/ppermute | solution.py:213
  87.4 6.8 %collective-permute-start.19 = (bf16[10,32,128]{2,1,0:T(8,128)(2,1)}, bf16[10,32,128]{2,1,0:T(8,128)(2,1)S(1)}, u32[]{:S(2)}, u32[]{:S(2)}) collective-permute-start(bf16[10,32,128]{2,1,0:T(8,128)(2,1)} %get-tuple-element.48), channel_id=1, source_target_pairs={{0,3},{1,4},{2,5},{3,6},{4,7},{5,0},{6,1},{7,2},{8,11},{9,12},{10,... | collective-permute-start | bytes 245768 | tf_op jit(solution)/shard_map/ppermute | solution.py:213
  94.2 5.6 %collective-permute-start.20 = (bf16[10,32,128]{2,1,0:T(8,128)(2,1)}, bf16[10,32,128]{2,1,0:T(8,128)(2,1)S(1)}, u32[]{:S(2)}, u32[]{:S(2)}) collective-permute-start(bf16[10,32,128]{2,1,0:T(8,128)(2,1)} %get-tuple-element.49), channel_id=1, source_target_pairs={{0,4},{1,5},{2,6},{3,7},{4,0},{5,1},{6,2},{7,3},{8,12},{9,13},{10,... | collective-permute-start | bytes 245768 | tf_op jit(solution)/shard_map/ppermute | solution.py:213
  99.8 5.6 %collective-permute-start.21 = (bf16[10,32,128]{2,1,0:T(8,128)(2,1)}, bf16[10,32,128]{2,1,0:T(8,128)(2,1)S(1)}, u32[]{:S(2)}, u32[]{:S(2)}) collective-permute-start(bf16[10,32,128]{2,1,0:T(8,128)(2,1)} %get-tuple-element.50), channel_id=1, source_target_pairs={{0,5},{1,6},{2,7},{3,0},{4,1},{5,2},{6,3},{7,4},{8,13},{9,14},{10,... | collective-permute-start | bytes 245768 | tf_op jit(solution)/shard_map/ppermute | solution.py:213
  105.4 5.7 %collective-permute-start.22 = (bf16[10,32,128]{2,1,0:T(8,128)(2,1)}, bf16[10,32,128]{2,1,0:T(8,128)(2,1)S(1)}, u32[]{:S(2)}, u32[]{:S(2)}) collective-permute-start(bf16[10,32,128]{2,1,0:T(8,128)(2,1)} %get-tuple-element.51), channel_id=1, source_target_pairs={{0,6},{1,7},{2,0},{3,1},{4,2},{5,3},{6,4},{7,5},{8,14},{9,15},{10,... | collective-permute-start | bytes 245768 | tf_op jit(solution)/shard_map/ppermute | solution.py:213
  111.1 5.5 %collective-permute-start.23 = (bf16[10,32,128]{2,1,0:T(8,128)(2,1)}, bf16[10,32,128]{2,1,0:T(8,128)(2,1)S(1)}, u32[]{:S(2)}, u32[]{:S(2)}) collective-permute-start(bf16[10,32,128]{2,1,0:T(8,128)(2,1)} %get-tuple-element.52), channel_id=1, source_target_pairs={{0,7},{1,0},{2,1},{3,2},{4,3},{5,4},{6,5},{7,6},{8,15},{9,8},{10,9... | collective-permute-start | bytes 245768 | tf_op jit(solution)/shard_map/ppermute | solution.py:213
  116.6 3.0 %copy-start.2 = (bf16[8,10,32,128]{3,2,1,0:T(8,128)(2,1)}, bf16[8,10,32,128]{3,2,1,0:T(8,128)(2,1)S(1)}, u32[]{:S(2)}) copy-start(bf16[8,10,32,128]{3,2,1,0:T(8,128)(2,1)S(1)} %bitcast_dynamic-update-slice_fusion.8.rest_2_) | copy-start | bytes 1966084
  116.6 3.0 %collective-permute-start.24 = (bf16[8,10,32,128]{3,2,1,0:T(8,128)(2,1)S(1)}, bf16[8,10,32,128]{3,2,1,0:T(8,128)(2,1)S(1)}, u32[]{:S(2)}, u32[]{:S(2)}) collective-permute-start(bf16[8,10,32,128]{3,2,1,0:T(8,128)(2,1)S(1)} %bitcast_dynamic-update-slice_fusion.8.rest_2_), channel_id=1, source_target_pairs={{0,8},{8,0},{1,9},{9,1},{2,10},{10,2},{3,11},{11,3},{4,12},{12,4},... | collective-permute-start | bytes 1966088 | tf_op jit(solution)/shard_map/ppermute | solution.py:240
  118.7 27.0 %collective-permute-start.16 = (bf16[8,6,32,128]{3,2,1,0:T(8,128)(2,1)}, bf16[8,6,32,128]{3,2,1,0:T(8,128)(2,1)}, u32[]{:S(2)}, u32[]{:S(2)}) collective-permute-start(bf16[8,6,32,128]{3,2,1,0:T(8,128)(2,1)} %constant_dynamic-update-slice_fusion.rest_2_), channel_id=1, source_target_pairs={{0,8},{8,0},{1,9},{9,1},{2,10},{10,2},{3,11},{11,3},{4,12},{12,4},... | collective-permute-start | bytes 1179656 | tf_op jit(solution)/shard_map/ppermute | solution.py:240
  119.6 1.0 copy-start.1
  120.5 0.8 copy-start.3
